TPU v7x, 32 devices: a whole 2x2x4 slice. The times are simulated.
32 devices in a mesh: grp: 2 (over x), node: 16 (over z, y, core).
Axes of the slice: x: 2, y: 2, z: 4, core: 2. Of those that a mesh axis runs over, the one named last changes fastest.
Arguments:
- grid_inputs: bfloat16 [32768, 474], P(('grp', 'node')), parts along dimension 0, may hold values from -6 to 6
- mesh_latent: bfloat16 [512, 512], P(('grp', 'node')), parts along dimension 0, may hold values from -6 to 6
- sender_ids: int32 [65536], P(('grp', 'node')), parts along dimension 0, may hold values from 0 to 1023
- receiver_ids: int32 [65536], P(('grp', 'node')), parts along dimension 0, may hold values from 0 to 255
- embed_weight: bfloat16 [474, 512], replicated, may hold values from -0.25 to 0.25
- sender_weight: bfloat16 [512, 512], replicated, may hold values from -0.25 to 0.25
- receiver_weight: bfloat16 [512, 512], replicated, may hold values from -0.25 to 0.25
- message_weight: bfloat16 [512, 512], replicated, may hold values from -0.25 to 0.25
- norm_gain: float32 [512], replicated, may hold values from 0.25 to 1.75
- out_grad: bfloat16 [512, 512], P(('grp', 'node')), parts along dimension 0, may hold values from -6 to 6
Outputs:
- mesh_update: bfloat16 [512, 512], P(('grp', 'node')), parts along dimension 0
- mesh_grad: bfloat16 [512, 512], P(('grp', 'node')), parts along dimension 0
- message_grad: float32 [1024, 512], P('grp'), parts along dimension 0
There are 2 independent parts, one for each index of `grp`. A program takes and returns all parts, laid end to end along the dimension named above; an argument that names none is the same for every part. Nothing has to cross between parts.
All inputs are finite; a program needn't handle non-finite values.
Results may differ from a plain program's by a relative error of at most 0.0052.
Values may be sent and summed in bfloat16 or wider, within the bound.
A program may use at most 64 MiB of HBM per device.

v0:
```python
import math

import jax
import jax.numpy as jnp
from jax import lax
from jax.sharding import PartitionSpec as P


def shards(
    grid_inputs,
    mesh_latent,
    sender_ids,
    receiver_ids,
    embed_weight,
    sender_weight,
    receiver_weight,
    message_weight,
    norm_gain,
    out_grad,
):
    n = lax.axis_size("node")
    owned = mesh_latent.shape[0]
    me = lax.axis_index("node")
    gathered = lax.all_gather(jnp.concatenate([mesh_latent, out_grad], axis=1), "node", axis=0, tiled=True)
    width = mesh_latent.shape[1]
    all_latent, all_grad = gathered[:, :width], gathered[:, width:]
    grid_latent = jax.nn.silu(
        jnp.dot(grid_inputs, embed_weight, preferred_element_type=jnp.float32)
    ).astype(jnp.bfloat16)
    send_term = jnp.dot(grid_latent, sender_weight, preferred_element_type=jnp.float32).astype(jnp.bfloat16)
    recv_term = jnp.dot(all_latent, receiver_weight, preferred_element_type=jnp.float32).astype(jnp.bfloat16)
    nodes = jnp.arange(owned * n, dtype=jnp.int32)
    by_sender = (sender_ids[:, None] == jnp.arange(grid_inputs.shape[0], dtype=jnp.int32)[None, :]).astype(jnp.bfloat16)
    by_receiver = (receiver_ids[:, None] == nodes[None, :]).astype(jnp.bfloat16)
    to_receiver = (nodes[:, None] == receiver_ids[None, :]).astype(jnp.bfloat16)
    preact = jnp.dot(by_sender, send_term, preferred_element_type=jnp.float32) + jnp.dot(
        by_receiver, recv_term, preferred_element_type=jnp.float32
    )
    gates = jax.nn.sigmoid(preact)
    hidden = (preact * gates).astype(jnp.bfloat16)
    slope = (gates * (1.0 + preact * (1.0 - gates))).astype(jnp.bfloat16)
    part = jnp.dot(to_receiver, jnp.concatenate([hidden, slope], axis=1), preferred_element_type=jnp.float32)
    both = lax.psum_scatter(part, "node", scatter_dimension=0, tiled=True)
    own_slope = both[:, width:]
    hidden_sum = lax.all_gather(both[:, :width].astype(jnp.bfloat16), "node", axis=0, tiled=True)
    summed = jnp.dot(hidden_sum, message_weight, preferred_element_type=jnp.float32)
    inverse = lax.rsqrt(jnp.mean(summed * summed, axis=-1, keepdims=True) + 1e-05)
    normed = summed * inverse
    upstream = all_grad.astype(jnp.float32)
    dnorm = upstream * norm_gain
    agg_grad = (
        inverse * (dnorm - normed * jnp.mean(dnorm * normed, axis=-1, keepdims=True))
    ).astype(jnp.bfloat16)
    own_normed = lax.dynamic_slice_in_dim(normed, me * owned, owned, 0)
    own_agg = lax.dynamic_slice_in_dim(agg_grad, me * owned, owned, 0)
    mesh_update = (mesh_latent.astype(jnp.float32) + own_normed * norm_gain).astype(jnp.bfloat16)
    hidden_grad = lax.dot_general(
        own_agg, message_weight, (((1,), (1,)), ((), ())), preferred_element_type=jnp.float32
    )
    recv_grad = (hidden_grad * own_slope).astype(jnp.bfloat16)
    mesh_grad = (
        out_grad.astype(jnp.float32)
        + lax.dot_general(
            recv_grad, receiver_weight, (((1,), (1,)), ((), ())), preferred_element_type=jnp.float32
        )
    ).astype(jnp.bfloat16)
    edge_total = receiver_ids.shape[0] * n
    message_grad = lax.dot_general(
        hidden_sum, agg_grad, (((0,), (0,)), ((), ())), preferred_element_type=jnp.float32
    ) / math.sqrt(edge_total)
    return (mesh_update, mesh_grad, message_grad)


def solution(mesh):
    placed = (
        P(("grp", "node"), None),
        P(("grp", "node"), None),
        P(("grp", "node")),
        P(("grp", "node")),
        P(),
        P(),
        P(),
        P(),
        P(),
        P(("grp", "node"), None),
    )
    return jax.shard_map(
        shards,
        mesh=mesh,
        in_specs=placed,
        out_specs=(P(("grp", "node"), None), P(("grp", "node"), None), P("grp", None)),
        check_vma=False,
    )
```

profile of v0, /device:TPU:1, one launch (start us, length us, event | category | flops | bytes accessed | tf_op | source)
XLA Modules:
  0.0 138.7 jit_solution(16257517477717786153)
XLA Ops:
  7.2 0.0 copy-start
  7.2 0.0 copy-start.8
  7.2 0.0 reduce-scatter.2.cloned.1.call-start
  7.2 0.8 pad_maximum_fusion
  8.0 25.9 %all_gather.6 = bf16[256,1024]{1,0:T(8,128)(2,1)} all-gather(bf16[16,1024]{1,0:T(8,128)(2,1)S(1)} %pad_maximum_fusion), channel_id=1, replica_groups=mesh['grp'=2,'node'=16] {'node'}, dimensions={0}, use_global_device_ids=true | all-gather | bytes 557056 | tf_op jit(solution)/shard_map/all_gather | solution.py:24
  34.0 0.0 copy-done
  34.0 1.8 %fusion.22 = f32[1024,512]{1,0:T(8,128)S(1)} fusion(bf16[1024,474]{0,1:T(8,128)(2,1)S(1)} %copy-done, bf16[474,512]{1,0:T(8,128)(2,1)} %param.14), kind=kOutput, calls=%fused_computation.39 | convolution fusion | flops 497025024 | bytes 3553280 | tf_op jit(solution)/shard_map/dot_general | solution.py:28
  35.8 0.0 copy-done.8
  35.8 0.0 copy-start.9
  35.8 6.1 %fusion = f32[2048,512]{0,1:T(8,128)} fusion(s32[2048]{0:T(1024)S(1)} %copy-done.8, bf16[512,512]{1,0:T(8,128)(2,1)} %param.15, f32[1024,512]{1,0:T(8,128)S(1)} %fusion.22), kind=kOutput, calls=%fused_computation.1 | convolution fusion | flops 2689597440 | bytes 6823936 | tf_op jit(solution)/shard_map/dot_general | solution.py:36
  41.9 0.0 copy-done.9
  41.9 5.9 %multiply_convert_fusion.1 = (bf16[2048,512]{0,1:T(8,128)(2,1)}, bf16[2048,512]{0,1:T(8,128)(2,1)}) fusion(f32[2048,512]{0,1:T(8,128)} %fusion, bf16[512,512]{1,0:T(8,128)(2,1)} %param.16, bf16[256,1024]{1,0:T(8,128)(2,1)} %all_gather.6, s32[2048]{0:T(1024)S(1)} %copy-done.9), kind=kOutput, calls=%fused_computation.7 | convolution fusion | flops 683278336 | bytes 9183232 | tf_op jit(solution)/shard_map/dot_general | solution.py:36
  47.8 4.5 %fusion.1 = f32[256,1024]{1,0:T(8,128)} fusion(bf16[2048,512]{0,1:T(8,128)(2,1)} %get-tuple-element.6, bf16[2048,512]{0,1:T(8,128)(2,1)} %get-tuple-element.5, s32[2048]{0:T(1024)S(1)} %copy-done.9), kind=kOutput, calls=%fused_computation.2 | convolution fusion | flops 1082654720 | bytes 5251072 | tf_op jit(solution)/shard_map/dot_general | solution.py:42
  52.3 0.0 reduce-scatter.2.cloned.1.call-update
  52.4 52.5 %reduce-scatter.2.cloned.1.call-done = f32[16,1024]{1,0:T(8,128)} async-done(((f32[256,1024]{1,0:T(8,128)}), f32[16,1024]{1,0:T(8,128)}) %reduce-scatter.2.cloned.1.call-update) | async-done | bytes 65552 | tf_op jit(solution)/shard_map/reduce_scatter | solution.py:43
  104.8 0.8 slice.31
  105.6 22.5 %all_gather.7 = bf16[256,512]{1,0:T(8,128)(2,1)S(1)} all-gather(bf16[16,512]{1,0:T(8,128)(2,1)S(1)} %slice.31), channel_id=1, replica_groups=mesh['grp'=2,'node'=16] {'node'}, dimensions={0}, use_global_device_ids=true | all-gather | bytes 278528 | tf_op jit(solution)/shard_map/all_gather | solution.py:45
  128.1 0.0 copy-done.1
  128.1 0.4 multiply_reduce_fusion.1
  128.4 0.0 copy-start.5
  128.5 0.0 copy-start.3
  128.5 0.0 copy-start.4
  128.5 0.0 copy-start.6
  128.5 0.0 copy-done.2
  128.5 0.0 copy-done.7
  128.5 0.2 multiply_reduce_fusion
  128.7 0.2 multiply_convert_fusion.6
  128.9 1.3 convolution_multiply_fusion
  130.2 0.0 copy-done.5
  130.2 0.6 add_convert_fusion
  130.8 0.0 copy-done.3
  130.8 1.0 fusion.7
  (7 shorter events, 0.0 us)
Async XLA Ops:
  7.2 26.8 %copy-start = (bf16[1024,474]{0,1:T(8,128)(2,1)S(1)}, bf16[1024,474]{0,1:T(8,128)(2,1)}, u32[]{:S(2)}) copy-start(bf16[1024,474]{0,1:T(8,128)(2,1)} %param.10) | copy-start | bytes 2912260
  7.2 28.6 %copy-start.8 = (s32[2048]{0:T(1024)S(1)}, s32[2048]{0:T(1024)}, u32[]{:S(2)}) copy-start(s32[2048]{0:T(1024)} %param.12) | copy-start | bytes 24580
  7.2 97.6 %reduce-scatter.2.cloned.1.call-start = ((), (), s32[]{:S(2)}) async-start(), calls=%async_computation.1 | async-start | bytes 1114112 | tf_op jit(solution)/shard_map/reduce_scatter | solution.py:43
  35.8 6.1 %copy-start.9 = (s32[2048]{0:T(1024)S(1)}, s32[2048]{0:T(1024)}, u32[]{:S(2)}) copy-start(s32[2048]{0:T(1024)} %param.13) | copy-start | bytes 24580
  47.8 80.3 %copy-start.1 = (bf16[512,512]{1,0:T(8,128)(2,1)S(1)}, bf16[512,512]{1,0:T(8,128)(2,1)}, u32[]{:S(2)}) copy-start(bf16[512,512]{1,0:T(8,128)(2,1)} %param.17) | copy-start | bytes 1572868
  52.3 76.2 %copy-start.2 = (bf16[256,1024]{1,0:T(8,128)(2,1)S(1)}, bf16[256,1024]{1,0:T(8,128)(2,1)}, u32[]{:S(2)}) copy-start(bf16[256,1024]{1,0:T(8,128)(2,1)} %all_gather.6) | copy-start | bytes 1572868
  52.3 76.2 %copy-start.7 = (f32[512]{0:T(512)S(1)}, f32[512]{0:T(512)}, u32[]{:S(2)}) copy-start(f32[512]{0:T(512)} %param.18) | copy-start | bytes 6148
  128.4 1.8 %copy-start.5 = (bf16[16,512]{1,0:T(8,128)(2,1)S(1)}, bf16[16,512]{1,0:T(8,128)(2,1)}, u32[]{:S(2)}) copy-start(bf16[16,512]{1,0:T(8,128)(2,1)} %param.11) | copy-start | bytes 49156
  128.5 2.4 %copy-start.3 = (bf16[512,512]{1,0:T(8,128)(2,1)S(1)}, bf16[512,512]{1,0:T(8,128)(2,1)}, u32[]{:S(2)}) copy-start(bf16[512,512]{1,0:T(8,128)(2,1)} %param.16) | copy-start | bytes 1572868
  128.5 2.4 %copy-start.4 = (bf16[16,512]{1,0:T(8,128)(2,1)S(1)}, bf16[16,512]{1,0:T(8,128)(2,1)}, u32[]{:S(2)}) copy-start(bf16[16,512]{1,0:T(8,128)(2,1)} %param.19) | copy-start | bytes 49156
  128.5 2.4 %copy-start.6 = (f32[16,1024]{1,0:T(8,128)S(1)}, f32[16,1024]{1,0:T(8,128)}, u32[]{:S(2)}) copy-start(f32[16,1024]{1,0:T(8,128)} %reduce-scatter.2.cloned.1.call-done) | copy-start | bytes 196612
Sparse Core Ops, SparseCore 0:
  52.5 52.3 reduce-scatter.1
where the time goes:
time: 139 us
  waiting for transfers between devices  52.5 us (38%)
  blocking collectives  48.4 us (35%)
  matrix products  21 us (15%)
  between operations  14.1 us (10%)
  other arithmetic  1.81 us (1%)
    reduce_scatter x1, waiting for transfers between devices, shards(): both = lax.psum_scatter(part, 'node', scatter_dimension=0, tiled=True)  52.5 us
    all_gather x1, blocking collectives, shards(): lax.all_gather(jnp.concatenate([mesh_latent, out_grad], axis=1), 'node',...  25.9 us
    all_gather x1, blocking collectives, shards(): lax.all_gather(both[:, :width].astype(jnp.bfloat16), 'node', axis=0, tile...  22.5 us
    dot_general x1, matrix products, shards(): jnp.dot(by_sender, send_term, preferred_element_type=jnp.float32)  6.09 us
    dot_general x1, matrix products, shards(): jnp.dot(by_receiver, recv_term, preferred_element_type=jnp.float32)  5.9 us
    dot_general x1, matrix products, shards(): jnp.dot(to_receiver, jnp.concatenate([hidden, slope], axis=1), preferred_...  4.54 us
  transfers between devices with their start and end apart: 1, of which 1 were waited for; matrix products, arithmetic and copies ran while one was open for 0% of the time, Pallas kernels for 0%

commit v1 on v0

v1 whole, which is shorter than its diff:
```python
import functools
import math

import jax
import jax.numpy as jnp
from jax import lax
from jax.experimental import pallas as pl
from jax.experimental.pallas import tpu as pltpu
from jax.sharding import PartitionSpec as P

LOGICAL = pl.DeviceIdType.MESH
F32 = jnp.float32
BF16 = jnp.bfloat16
CHUNK = 512
LANES = 128


def dot_nn(a, b):
    return jnp.dot(a, b, preferred_element_type=F32)


def dot_nt(a, b):
    return lax.dot_general(a, b, (((1,), (1,)), ((), ())), preferred_element_type=F32)


def dot_tn(a, b):
    return lax.dot_general(a, b, (((0,), (0,)), ((), ())), preferred_element_type=F32)


def selector(ids_row, columns):
    column = jnp.broadcast_to(ids_row, (LANES, LANES)).T
    lane = lax.broadcasted_iota(jnp.int32, (LANES, LANES), 1)
    parts = [
        jnp.where(column == lane + start, 1.0, 0.0).astype(BF16)
        for start in range(0, columns, LANES)
    ]
    return jnp.concatenate(parts, axis=1)


def kernel(
    chips,
    edge_total,
    grid_ref,
    latent_ref,
    sender_ref,
    receiver_ref,
    embed_ref,
    sendw_ref,
    recvw_ref,
    messw_ref,
    gain_ref,
    grad_ref,
    update_ref,
    meshgrad_ref,
    weight_ref,
    latents,
    grads,
    hsums,
    table,
    rtable,
    picked,
    picks,
    rpicks,
    acc,
    outgoing,
    pair_in,
    chip_sum,
    peer_in,
    send_ici,
    recv_ici,
    send_core,
    recv_core,
    pair_send,
    pair_recv,
    peer_send,
    peer_recv,
):
    grp = lax.axis_index("grp")
    me = lax.axis_index("node")
    chip = me // 2
    core = me % 2
    other = 1 - core
    partner = (grp, chip * 2 + other)
    owned, width = latent_ref.shape
    half = chips * owned
    nodes = 2 * half
    sub_rows = sender_ref.shape[0]
    shift = owned.bit_length() - 1

    def peer(k):
        return lax.rem(chip + k, chips)

    barrier = pltpu.get_barrier_semaphore()

    def greet(k, carry):
        pl.semaphore_signal(barrier, inc=1, device_id=(grp, peer(k) * 2 + core), device_id_type=LOGICAL)
        return carry

    lax.fori_loop(1, chips, greet, 0)
    pl.semaphore_signal(barrier, inc=1, device_id=partner, device_id_type=LOGICAL)
    latents[core, chip] = latent_ref[...]
    grads[core, chip] = grad_ref[...]
    pl.semaphore_wait(barrier, chips)

    def spread_copy(slot, buffer, source, target):
        return pltpu.make_async_remote_copy(
            src_ref=buffer.at[core, source],
            dst_ref=buffer.at[core, source],
            send_sem=send_ici.at[slot, target],
            recv_sem=recv_ici.at[slot, source],
            device_id=(grp, target * 2 + core),
            device_id_type=LOGICAL,
        )

    def core_copy(slot, buffer, block, side):
        return pltpu.make_async_remote_copy(
            src_ref=buffer.at[side, block],
            dst_ref=buffer.at[side, block],
            send_sem=send_core.at[slot, block],
            recv_sem=recv_core.at[slot, block],
            device_id=partner,
            device_id_type=LOGICAL,
        )

    def spread_start(slot, buffer):
        def body(k, carry):
            spread_copy(slot, buffer, chip, peer(k)).start()
            return carry

        lax.fori_loop(1, chips, body, 0)
        core_copy(slot, buffer, chip, core).start()

    def spread_forward(slot, buffer):
        def body(k, carry):
            j = peer(chips - k)
            spread_copy(slot, buffer, j, j).wait_recv()
            core_copy(slot, buffer, j, core).start()
            return carry

        lax.fori_loop(1, chips, body, 0)

    def spread_finish(slot, buffer):
        def body(k, carry):
            j = peer(chips - k)
            core_copy(slot, buffer, j, other).wait_recv()
            return carry

        lax.fori_loop(0, chips, body, 0)

    def spread_drain(slot, buffer):
        def body(k, carry):
            spread_copy(slot, buffer, chip, peer(k)).wait_send()
            return carry

        def body_core(k, carry):
            core_copy(slot, buffer, peer(k), core).wait_send()
            return carry

        lax.fori_loop(1, chips, body, 0)
        lax.fori_loop(0, chips, body_core, 0)

    spread_start(0, latents)
    spread_start(1, grads)

    embedded = dot_nn(grid_ref[...], embed_ref[...])
    embedded = (embedded * (0.5 * jnp.tanh(0.5 * embedded) + 0.5)).astype(BF16)
    table[...] = dot_nn(embedded, sendw_ref[...]).astype(BF16)
    spread_forward(0, latents)

    per_chunk = CHUNK // LANES

    def pick_senders(step, carry):
        for b in range(per_chunk):
            ids = sender_ref[pl.ds(step * per_chunk + b, 1), :]
            picks[b * LANES : (b + 1) * LANES, :] = selector(ids, picks.shape[1])
        rows = pl.ds(pl.multiple_of(step * CHUNK, CHUNK), CHUNK)
        picked[rows, :] = dot_nn(picks[...], table[...])
        return carry

    lax.fori_loop(0, sub_rows // per_chunk, pick_senders, 0)

    spread_finish(0, latents)
    rtable[...] = dot_nn(latents[...].reshape(nodes, width), recvw_ref[...]).astype(BF16)
    acc[...] = jnp.zeros_like(acc)
    spread_forward(1, grads)

    def sum_edges(step, carry):
        row_parts = []
        for b in range(per_chunk):
            ids = receiver_ref[pl.ds(step * per_chunk + b, 1), :]
            owner = lax.shift_right_logical(ids, shift)
            place = (owner & 1) * half + lax.shift_right_logical(owner, 1) * owned + (ids & (owned - 1))
            rpicks[b * LANES : (b + 1) * LANES, :] = selector(place, nodes)
            row_parts.append(place)
        places = jnp.concatenate(row_parts, axis=1)
        rows = pl.ds(pl.multiple_of(step * CHUNK, CHUNK), CHUNK)
        preact = picked[rows, :] + dot_nn(rpicks[...], rtable[...])
        gates = 0.5 * jnp.tanh(0.5 * preact) + 0.5
        hidden = preact * gates
        slope = gates + hidden * (1.0 - gates)
        position = lax.broadcasted_iota(jnp.int32, (nodes, CHUNK), 0)
        spreader = jnp.where(position == places, 1.0, 0.0).astype(BF16)
        acc[0] += dot_nn(spreader, hidden.astype(BF16)).reshape(2, chips, owned, width)
        acc[1] += dot_nn(spreader, slope.astype(BF16)).reshape(2, chips, owned, width)
        return carry

    lax.fori_loop(0, sub_rows // per_chunk, sum_edges, 0)

    def pair_copy(kind):
        return pltpu.make_async_remote_copy(
            src_ref=outgoing.at[kind],
            dst_ref=pair_in.at[kind],
            send_sem=pair_send.at[kind],
            recv_sem=pair_recv.at[kind],
            device_id=partner,
            device_id_type=LOGICAL,
        )

    def peer_copy(kind, block, source, target):
        return pltpu.make_async_remote_copy(
            src_ref=chip_sum.at[kind, block],
            dst_ref=peer_in.at[kind, source],
            send_sem=peer_send.at[kind, target],
            recv_sem=peer_recv.at[kind, source],
            device_id=(grp, target * 2 + core),
            device_id_type=LOGICAL,
        )

    for kind in range(2):
        outgoing[kind] = acc[kind, other].astype(BF16)
        pair_copy(kind).start()
    for kind in range(2):
        pair_copy(kind).wait_recv()
        total = acc[kind, core] + pair_in[kind].astype(F32)
        acc[kind, core] = total
        chip_sum[kind] = total.astype(BF16)

        def send(k, carry, kind=kind):
            j = peer(k)
            peer_copy(kind, j, chip, j).start()
            return carry

        lax.fori_loop(1, chips, send, 0)

    def collect(kind):
        def body(k, total):
            j = peer(chips - k)
            peer_copy(kind, j, j, j).wait_recv()
            return total + peer_in[kind, j].astype(F32)

        return lax.fori_loop(1, chips, body, acc[kind, core, chip])

    def normalise(rows, upstream):
        summed = dot_nn(rows, messw_ref[...])
        inverse = lax.rsqrt(jnp.mean(summed * summed, axis=-1, keepdims=True) + 1e-05)
        normed = summed * inverse
        dnorm = upstream.astype(F32) * gain_ref[...]
        agg = (inverse * (dnorm - normed * jnp.mean(dnorm * normed, axis=-1, keepdims=True))).astype(BF16)
        return normed, agg

    own_hidden = collect(0).astype(BF16)
    hsums[core, chip] = own_hidden
    spread_start(2, hsums)
    normed, agg = normalise(own_hidden, grad_ref[...])
    update_ref[...] = (latent_ref[...].astype(F32) + normed * gain_ref[...]).astype(BF16)
    hidden_grad = dot_nt(agg, messw_ref[...])
    spread_forward(2, hsums)
    recv_grad = (hidden_grad * collect(1)).astype(BF16)
    meshgrad_ref[...] = (grad_ref[...].astype(F32) + dot_nt(recv_grad, recvw_ref[...])).astype(BF16)
    spread_finish(1, grads)
    spread_finish(2, hsums)
    every = hsums[...].reshape(nodes, width)
    _, all_agg = normalise(every, grads[...].reshape(nodes, width))
    weight_ref[...] = dot_tn(every, all_agg) * (1.0 / math.sqrt(edge_total))

    spread_drain(0, latents)
    spread_drain(1, grads)
    spread_drain(2, hsums)
    for kind in range(2):
        pair_copy(kind).wait_send()

        def drain(k, carry, kind=kind):
            j = peer(k)
            peer_copy(kind, j, chip, j).wait_send()
            return carry

        lax.fori_loop(1, chips, drain, 0)


def shards(
    grid_inputs,
    mesh_latent,
    sender_ids,
    receiver_ids,
    embed_weight,
    sender_weight,
    receiver_weight,
    message_weight,
    norm_gain,
    out_grad,
):
    n = lax.axis_size("node")
    chips = n // 2
    owned, width = mesh_latent.shape
    edges = sender_ids.shape[0]
    senders = grid_inputs.shape[0]
    half = chips * owned
    nodes = 2 * half
    vmem = pl.BlockSpec(memory_space=pltpu.VMEM)
    dma = pltpu.SemaphoreType.DMA
    return pl.pallas_call(
        functools.partial(kernel, chips, edges * n),
        out_shape=(
            jax.ShapeDtypeStruct((owned, width), BF16),
            jax.ShapeDtypeStruct((owned, width), BF16),
            jax.ShapeDtypeStruct((width, width), F32),
        ),
        in_specs=[vmem] * 10,
        out_specs=(vmem, vmem, vmem),
        scratch_shapes=[
            pltpu.VMEM((2, chips, owned, width), BF16),
            pltpu.VMEM((2, chips, owned, width), BF16),
            pltpu.VMEM((2, chips, owned, width), BF16),
            pltpu.VMEM((senders, width), BF16),
            pltpu.VMEM((nodes, width), BF16),
            pltpu.VMEM((edges, width), F32),
            pltpu.VMEM((CHUNK, senders), BF16),
            pltpu.VMEM((CHUNK, nodes), BF16),
            pltpu.VMEM((2, 2, chips, owned, width), F32),
            pltpu.VMEM((2, chips, owned, width), BF16),
            pltpu.VMEM((2, chips, owned, width), BF16),
            pltpu.VMEM((2, chips, owned, width), BF16),
            pltpu.VMEM((2, chips, owned, width), BF16),
            dma((3, chips)),
            dma((3, chips)),
            dma((3, chips)),
            dma((3, chips)),
            dma((2,)),
            dma((2,)),
            dma((2, chips)),
            dma((2, chips)),
        ],
        compiler_params=pltpu.CompilerParams(
            collective_id=0, has_side_effects=True, vmem_limit_bytes=56 * 1024 * 1024
        ),
    )(
        grid_inputs,
        mesh_latent,
        sender_ids.reshape(edges // LANES, LANES),
        receiver_ids.reshape(edges // LANES, LANES),
        embed_weight,
        sender_weight,
        receiver_weight,
        message_weight,
        norm_gain.reshape(1, width),
        out_grad,
    )


def solution(mesh):
    placed = (
        P(("grp", "node"), None),
        P(("grp", "node"), None),
        P(("grp", "node")),
        P(("grp", "node")),
        P(),
        P(),
        P(),
        P(),
        P(),
        P(("grp", "node"), None),
    )
    return jax.shard_map(
        shards,
        mesh=mesh,
        in_specs=placed,
        out_specs=(P(("grp", "node"), None), P(("grp", "node"), None), P("grp", None)),
        check_vma=False,
    )
```

time: 139 us -> 43.4 us (0.31)
  waiting for transfers between devices: 52.5 us -> 0 us
  blocking collectives: 48.4 us -> 0 us
  Pallas kernels: 0 us -> 36 us
  matrix products: 21 us -> 0 us
  between operations: 14.1 us -> 0.65 us
  local copies, waits for them, and re-layouts: 0.81 us -> 6.47 us
  other arithmetic: 1.81 us -> 0 us
    reduce_scatter x1 -> x0, waiting for transfers between devices: 52.5 us -> none  [shards(): both = lax.psum_scatter(part, 'node', scatter_dimension=0, tiled=True)]
    all_gather x2 -> x0, blocking collectives: 48.4 us -> none  [the longest x1 25.9 us: shards(): lax.all_gather(jnp.concatenate([mesh_latent, out_grad], axis=1), 'node',...]
    pallas_call x0 -> x1, Pallas kernels: none -> 36 us  [shards(): pl.pallas_call(functools.partial(kernel, chips, edges * n), out_shape=(ja...]
    dot_general x7 -> x0, matrix products: 21 us -> none  [the longest x1 6.09 us: shards(): jnp.dot(by_sender, send_term, preferred_element_type=jnp.float32)]
    unnamed x20 -> x6, local copies, waits for them, and re-layouts: 0.05 us -> 6.47 us
  transfers between devices with their start and end apart: 1 -> 0, of which waited for: 1 -> 0; matrix products, arithmetic and copies ran while one was open for 0% -> 0% of each run, Pallas kernels for 0% -> 0%
where the time goes in v1:
time: 43.4 us; the launch traced here: 43.1 us
  Pallas kernels  36 us (83%)
  local copies, waits for them, and re-layouts  6.47 us (15%)
  between operations  0.65 us (1%)
    pallas_call x1, Pallas kernels, shards(): pl.pallas_call(functools.partial(kernel, chips, edges * n), out_shape=(ja...  36 us
    unnamed x6, local copies, waits for them, and re-layouts  6.47 us

profile of v1, /device:TPU:1, one launch (start us, length us, event | category | flops | bytes accessed | tf_op | source)
XLA Modules:
  0.0 43.1 jit_solution(1942942064279979463)
XLA Ops:
  0.6 2.3 %copy.13.grid_ref = bf16[1024,474]{1,0:T(8,128)(2,1)} copy(bf16[1024,474]{0,1:T(8,128)(2,1)} %param.10) | data formatting | bytes 1941504 | tf_op args[0]
  2.9 36.0 %shard_map.121 = (bf16[16,512]{1,0:T(8,128)(2,1)}, bf16[16,512]{1,0:T(8,128)(2,1)}, f32[512,512]{1,0:T(8,128)}) custom-call(bf16[1024,474]{1,0:T(8,128)(2,1)} %copy.13.grid_ref, bf16[16,512]{1,0:T(8,128)(2,1)} %latent_ref.1, s32[16,128]{1,0:T(8,128)} %bitcast.3, s32[16,128]{1,0:T(8,128)} %bitcast.4, bf16[474,512]{1,0:T(8,128)(2,1)} %embed_ref.1, ...), custom_call_target="tpu_custom_call" | custom-call | tf_op jit(solution)/shard_map/pallas_call | solution.py:311
  38.9 0.0 copy-start
  38.9 1.3 %copy.17 = bf16[16,512]{1,0:T(8,128)(2,1)} copy(bf16[16,512]{1,0:T(8,128)(2,1)} %get-tuple-element.6) | data formatting | bytes 32768
  40.2 0.0 copy-done
  40.2 0.6 %copy.18 = bf16[16,512]{1,0:T(8,128)(2,1)} copy(bf16[16,512]{1,0:T(8,128)(2,1)S(1)} %copy-done) | data formatting | bytes 32768
  40.9 2.3 %copy.19 = f32[512,512]{1,0:T(8,128)} copy(f32[512,512]{1,0:T(8,128)} %get-tuple-element.8) | data formatting | bytes 2097152
Async XLA Ops:
  38.9 1.3 %copy-start = (bf16[16,512]{1,0:T(8,128)(2,1)S(1)}, bf16[16,512]{1,0:T(8,128)(2,1)}, u32[]{:S(2)}) copy-start(bf16[16,512]{1,0:T(8,128)(2,1)} %get-tuple-element.7) | copy-start | bytes 49156

commit v2 on v1

v2 whole, which is shorter than its diff:
```python
import functools
import math

import jax
import jax.numpy as jnp
from jax import lax
from jax.experimental import pallas as pl
from jax.experimental.pallas import tpu as pltpu
from jax.sharding import PartitionSpec as P

LOGICAL = pl.DeviceIdType.MESH
F32 = jnp.float32
BF16 = jnp.bfloat16
CHUNK = 512
LANES = 128


def dot_nn(a, b):
    return jnp.dot(a, b, preferred_element_type=F32)


def dot_nt(a, b):
    return lax.dot_general(a, b, (((1,), (1,)), ((), ())), preferred_element_type=F32)


def dot_tn(a, b):
    return lax.dot_general(a, b, (((0,), (0,)), ((), ())), preferred_element_type=F32)


def selector(ids_row, columns):
    column = jnp.broadcast_to(ids_row, (LANES, LANES)).T
    lane = lax.broadcasted_iota(jnp.int32, (LANES, LANES), 1)
    parts = [
        jnp.where(column == lane + start, 1.0, 0.0).astype(BF16)
        for start in range(0, columns, LANES)
    ]
    return jnp.concatenate(parts, axis=1)


def kernel(
    chips,
    grid_hbm,
    latent_ref,
    sender_hbm,
    receiver_hbm,
    embed_hbm,
    sendw_hbm,
    recvw_hbm,
    messw_hbm,
    gain_ref,
    grad_ref,
    update_ref,
    meshgrad_ref,
    hidden_ref,
    agg_ref,
    grid_ref,
    sender_ref,
    receiver_ref,
    embed_ref,
    sendw_ref,
    recvw_ref,
    messw_ref,
    latents,
    grads,
    hsums,
    table,
    rtable,
    picked,
    picks,
    rpicks,
    spreader,
    terms,
    acc,
    outgoing,
    pair_in,
    peer_out,
    peer_in,
    load_sem,
    send_ici,
    recv_ici,
    send_core,
    recv_core,
    pair_send,
    pair_recv,
    sum_send,
    sum_recv,
):
    grp = lax.axis_index("grp")
    me = lax.axis_index("node")
    chip = me // 2
    core = me % 2
    other = 1 - core
    owned, width = latent_ref.shape
    half = chips * owned
    nodes = 2 * half
    edges = terms.shape[1]
    shift = owned.bit_length() - 1

    def at(place, c):
        return (grp, place * 2 + c)

    partner = at(chip, other)

    def loop(low, body):
        def step(k, carry):
            body(lax.rem(chip + k, chips))
            return carry

        lax.fori_loop(low, chips, step, 0)

    barrier = pltpu.get_barrier_semaphore()

    def greet(target):
        pl.semaphore_signal(barrier, inc=1, device_id=target, device_id_type=LOGICAL)

    loop(1, lambda j: greet(at(j, core)))
    greet(partner)

    loads = [
        pltpu.make_async_copy(source, target, load_sem.at[i])
        for i, (source, target) in enumerate(
            (
                (embed_hbm, embed_ref),
                (grid_hbm, grid_ref),
                (sendw_hbm, sendw_ref),
                (sender_hbm, sender_ref),
                (receiver_hbm, receiver_ref),
                (recvw_hbm, recvw_ref),
                (messw_hbm, messw_ref),
            )
        )
    ]
    for load in loads:
        load.start()
    latents[core, chip] = latent_ref[...]
    grads[core, chip] = grad_ref[...]

    def chip_copy(slot, buffer, source, target):
        block = buffer.at[core, source]
        return pltpu.make_async_remote_copy(
            src_ref=block,
            dst_ref=block,
            send_sem=send_ici.at[slot, target],
            recv_sem=recv_ici.at[slot, source],
            device_id=at(target, core),
            device_id_type=LOGICAL,
        )

    def core_copy(slot, buffer, place, c):
        block = buffer.at[c, place]
        return pltpu.make_async_remote_copy(
            src_ref=block,
            dst_ref=block,
            send_sem=send_core.at[slot, place],
            recv_sem=recv_core.at[slot, place],
            device_id=partner,
            device_id_type=LOGICAL,
        )

    def spread_start(slot, buffer):
        loop(1, lambda j: chip_copy(slot, buffer, chip, j).start())
        core_copy(slot, buffer, chip, core).start()

    def spread_forward(slot, buffer):
        def body(j):
            chip_copy(slot, buffer, j, j).wait_recv()
            core_copy(slot, buffer, j, core).start()

        loop(1, body)

    def spread_finish(slot, buffer):
        loop(0, lambda j: core_copy(slot, buffer, j, other).wait_recv())

    def spread_drain(slot, buffer):
        loop(1, lambda j: chip_copy(slot, buffer, chip, j).wait_send())
        loop(0, lambda j: core_copy(slot, buffer, j, core).wait_send())

    def embed():
        loads[0].wait()
        loads[1].wait()
        embedded = dot_tn(grid_ref[...], embed_ref[...])
        embedded = (embedded * (0.5 * jnp.tanh(0.5 * embedded) + 0.5)).astype(BF16)
        loads[2].wait()
        table[...] = dot_nn(embedded, sendw_ref[...]).astype(BF16)

    pl.semaphore_wait(barrier, chips)
    spread_start(0, latents)
    embed()
    loads[3].wait()
    loads[4].wait()

    per_chunk = CHUNK // LANES

    def pick_senders(step, carry):
        position = lax.broadcasted_iota(jnp.int32, (nodes, LANES), 0)
        for b in range(per_chunk):
            row = pl.ds(step * per_chunk + b, 1)
            picks[b * LANES : (b + 1) * LANES, :] = selector(sender_ref[row, :], picks.shape[1])
            ids = receiver_ref[row, :]
            owner = lax.shift_right_logical(ids, shift)
            place = (owner & 1) * half + lax.shift_right_logical(owner, 1) * owned + (ids & (owned - 1))
            start = pl.multiple_of(step * CHUNK + b * LANES, LANES)
            rpicks[pl.ds(start, LANES), :] = selector(place, nodes)
            spreader[:, pl.ds(start, LANES)] = jnp.where(position == place, 1.0, 0.0).astype(BF16)
        rows = pl.ds(pl.multiple_of(step * CHUNK, CHUNK), CHUNK)
        picked[rows, :] = dot_nn(picks[...], table[...])
        return carry

    chunks = edges // CHUNK
    lax.fori_loop(0, chunks, pick_senders, 0)
    for load in loads[5:]:
        load.wait()
    spread_forward(0, latents)
    spread_start(1, grads)
    spread_finish(0, latents)
    rtable[...] = dot_nn(latents[...].reshape(nodes, width), recvw_ref[...]).astype(BF16)

    def read_edges(step, carry):
        rows = pl.ds(pl.multiple_of(step * CHUNK, CHUNK), CHUNK)
        preact = picked[rows, :] + dot_nn(rpicks[rows, :], rtable[...])
        gates = 0.5 * jnp.tanh(0.5 * preact) + 0.5
        hidden = preact * gates
        terms[0, rows, :] = hidden.astype(BF16)
        terms[1, rows, :] = (gates + hidden * (1.0 - gates)).astype(BF16)
        return carry

    lax.fori_loop(0, chunks, read_edges, 0)

    def pair_copy(kind):
        return pltpu.make_async_remote_copy(
            src_ref=outgoing.at[kind],
            dst_ref=pair_in.at[kind],
            send_sem=pair_send.at[kind],
            recv_sem=pair_recv.at[kind],
            device_id=partner,
            device_id_type=LOGICAL,
        )

    def sum_copy(kind, block, source, target):
        return pltpu.make_async_remote_copy(
            src_ref=peer_out.at[kind, block],
            dst_ref=peer_in.at[kind, source],
            send_sem=sum_send.at[kind, target],
            recv_sem=sum_recv.at[kind, source],
            device_id=at(target, core),
            device_id_type=LOGICAL,
        )

    def sums(kind, c):
        rows = spreader[pl.ds(pl.multiple_of(c * half, half), half), :]
        return dot_nn(rows, terms[kind])

    def pair_start(kind):
        outgoing[kind] = sums(kind, other).astype(BF16).reshape(chips, owned, width)
        pair_copy(kind).start()

    def own_sums(kind):
        acc[kind] = sums(kind, core).reshape(chips, owned, width)

    def sum_start(kind):
        pair_copy(kind).wait_recv()
        mine = acc[kind] + pair_in[kind].astype(F32)
        acc[kind] = mine
        peer_out[kind] = mine.astype(BF16)
        loop(1, lambda j: sum_copy(kind, j, chip, j).start())

    def collect(kind):
        def body(k, total):
            j = lax.rem(chip + k, chips)
            sum_copy(kind, j, j, j).wait_recv()
            return total + peer_in[kind, j].astype(F32)

        return lax.fori_loop(1, chips, body, acc[kind, chip])

    def normalise(rows, upstream):
        summed = dot_nn(rows, messw_ref[...])
        inverse = lax.rsqrt(jnp.mean(summed * summed, axis=-1, keepdims=True) + 1e-05)
        normed = summed * inverse
        dnorm = upstream.astype(F32) * gain_ref[...]
        agg = (inverse * (dnorm - normed * jnp.mean(dnorm * normed, axis=-1, keepdims=True))).astype(BF16)
        return normed, agg

    pair_start(0)
    own_sums(0)
    sum_start(0)
    pair_start(1)
    own_sums(1)
    sum_start(1)
    spread_forward(1, grads)
    own_hidden = collect(0).astype(BF16)
    hsums[core, chip] = own_hidden
    spread_start(2, hsums)
    normed, agg = normalise(own_hidden, grad_ref[...])
    update_ref[...] = (latent_ref[...].astype(F32) + normed * gain_ref[...]).astype(BF16)
    hidden_grad = dot_nt(agg, messw_ref[...])
    spread_forward(2, hsums)
    recv_grad = (hidden_grad * collect(1)).astype(BF16)
    meshgrad_ref[...] = (grad_ref[...].astype(F32) + dot_nt(recv_grad, recvw_ref[...])).astype(BF16)
    spread_finish(1, grads)
    spread_finish(2, hsums)
    every = hsums[...].reshape(nodes, width)
    hidden_ref[...] = every
    _, all_agg = normalise(every, grads[...].reshape(nodes, width))
    agg_ref[...] = all_agg

    spread_drain(0, latents)
    spread_drain(1, grads)
    spread_drain(2, hsums)
    for kind in range(2):
        pair_copy(kind).wait_send()
        loop(1, lambda j, kind=kind: sum_copy(kind, j, chip, j).wait_send())


def finish(scale, update_in, meshgrad_in, hidden_ref, agg_ref, update_ref, meshgrad_ref, weight_ref):
    update_ref[...] = update_in[...]
    meshgrad_ref[...] = meshgrad_in[...]
    weight_ref[...] = dot_tn(hidden_ref[...], agg_ref[...]) * scale


def shards(
    grid_inputs,
    mesh_latent,
    sender_ids,
    receiver_ids,
    embed_weight,
    sender_weight,
    receiver_weight,
    message_weight,
    norm_gain,
    out_grad,
):
    n = lax.axis_size("node")
    chips = n // 2
    owned, width = mesh_latent.shape
    edges = sender_ids.shape[0]
    senders, channels = grid_inputs.shape
    nodes = n * owned
    vmem = pl.BlockSpec(memory_space=pltpu.VMEM)
    hbm = pl.BlockSpec(memory_space=pl.ANY)
    dma = pltpu.SemaphoreType.DMA
    id_rows = (edges // LANES, LANES)
    blocks = (2, chips, owned, width)
    row = jax.ShapeDtypeStruct((owned, width), BF16)
    every = jax.ShapeDtypeStruct((nodes, width), BF16)
    update, mesh_grad, hidden, agg = pl.pallas_call(
        functools.partial(kernel, chips),
        out_shape=(row, row, every, every),
        in_specs=[hbm, vmem, hbm, hbm, hbm, hbm, hbm, hbm, vmem, vmem],
        out_specs=(vmem, vmem, vmem, vmem),
        scratch_shapes=[
            pltpu.VMEM((channels, senders), BF16),
            pltpu.VMEM(id_rows, jnp.int32),
            pltpu.VMEM(id_rows, jnp.int32),
            pltpu.VMEM(embed_weight.shape, BF16),
            pltpu.VMEM((width, width), BF16),
            pltpu.VMEM((width, width), BF16),
            pltpu.VMEM((width, width), BF16),
            pltpu.VMEM(blocks, BF16),
            pltpu.VMEM(blocks, BF16),
            pltpu.VMEM(blocks, BF16),
            pltpu.VMEM((senders, width), BF16),
            pltpu.VMEM((nodes, width), BF16),
            pltpu.VMEM((edges, width), F32),
            pltpu.VMEM((CHUNK, senders), BF16),
            pltpu.VMEM((edges, nodes), BF16),
            pltpu.VMEM((nodes, edges), BF16),
            pltpu.VMEM((2, edges, width), BF16),
            pltpu.VMEM(blocks, F32),
            pltpu.VMEM(blocks, BF16),
            pltpu.VMEM(blocks, BF16),
            pltpu.VMEM(blocks, BF16),
            pltpu.VMEM(blocks, BF16),
            dma((7,)),
            dma((3, chips)),
            dma((3, chips)),
            dma((3, chips)),
            dma((3, chips)),
            dma((2,)),
            dma((2,)),
            dma((2, chips)),
            dma((2, chips)),
        ],
        compiler_params=pltpu.CompilerParams(
            collective_id=0, has_side_effects=True, vmem_limit_bytes=58 * 1024 * 1024
        ),
    )(
        grid_inputs.T,
        mesh_latent,
        sender_ids.reshape(id_rows),
        receiver_ids.reshape(id_rows),
        embed_weight,
        sender_weight,
        receiver_weight,
        message_weight,
        norm_gain.reshape(1, width),
        out_grad,
    )
    return pl.pallas_call(
        functools.partial(finish, 1.0 / math.sqrt(edges * n)),
        out_shape=(row, row, jax.ShapeDtypeStruct((width, width), F32)),
        in_specs=[vmem] * 4,
        out_specs=(vmem, vmem, vmem),
    )(update, mesh_grad, hidden, agg)


def solution(mesh):
    placed = (
        P(("grp", "node"), None),
        P(("grp", "node"), None),
        P(("grp", "node")),
        P(("grp", "node")),
        P(),
        P(),
        P(),
        P(),
        P(),
        P(("grp", "node"), None),
    )
    return jax.shard_map(
        shards,
        mesh=mesh,
        in_specs=placed,
        out_specs=(P(("grp", "node"), None), P(("grp", "node"), None), P("grp", None)),
        check_vma=False,
    )
```

time: 43.4 us -> 33.3 us (0.77)
  local copies, waits for them, and re-layouts: 6.47 us -> 0 us
  Pallas kernels: 36 us -> 32.4 us
    unnamed x6 -> x0, local copies, waits for them, and re-layouts: 6.47 us -> none
    pallas_call x1 -> x2, Pallas kernels: 36 us -> 32.4 us  [the longest x1 30 us: shards(): pl.pallas_call(functools.partial(kernel, chips), out_shape=(row, row, eve...]
where the time goes in v2:
time: 33.3 us; the launch traced here: 33 us
  Pallas kernels  32.4 us (97%)
  between operations  0.64 us (2%)
    pallas_call x1, Pallas kernels, shards(): pl.pallas_call(functools.partial(kernel, chips), out_shape=(row, row, eve...  30 us
    pallas_call x1, Pallas kernels, shards(): pl.pallas_call(functools.partial(finish, 1.0 / math.sqrt(edges * n)), out...  2.36 us

profile of v2, /device:TPU:1, one launch (start us, length us, event | category | flops | bytes accessed | tf_op | source)
XLA Modules:
  0.0 33.0 jit_solution(15881816384745605441)
XLA Ops:
  0.6 30.0 %shard_map.121 = (bf16[16,512]{1,0:T(8,128)(2,1)}, bf16[16,512]{1,0:T(8,128)(2,1)}, bf16[256,512]{1,0:T(8,128)(2,1)}, bf16[256,512]{1,0:T(8,128)(2,1)}) custom-call(bf16[474,1024]{1,0:T(8,128)(2,1)} %bitcast.4, bf16[16,512]{1,0:T(8,128)(2,1)} %latent_ref.1, s32[16,128]{1,0:T(8,128)} %bitcast.5, s32[16,128]{1,0:T(8,128)} %bitcast.6, ...), custom_call_target="tpu_custom_call" | custom-call | tf_op jit(solution)/shard_map/pallas_call | solution.py:345
  30.7 2.4 %shard_map.122 = (bf16[16,512]{1,0:T(8,128)(2,1)}, bf16[16,512]{1,0:T(8,128)(2,1)}, f32[512,512]{1,0:T(8,128)}) custom-call(bf16[16,512]{1,0:T(8,128)(2,1)} %get-tuple-element.7.update_in, bf16[16,512]{1,0:T(8,128)(2,1)} %get-tuple-element.8.meshgrad_in, bf16[256,512]{1,0:T(8,128)(2,1)} %get-tuple-element.9.hidden_ref, ...), custom_call_target="tpu_custom_call" | custom-call | tf_op jit(solution)/shard_map/pallas_call | solution.py:398

commit v3 on v2

--- a/solution.py
+++ b/solution.py
@@ -40,15 +40,15 @@
 def kernel(
     chips,
     grid_hbm,
-    latent_ref,
+    latent_hbm,
     sender_hbm,
     receiver_hbm,
     embed_hbm,
     sendw_hbm,
     recvw_hbm,
     messw_hbm,
-    gain_ref,
-    grad_ref,
+    gain_hbm,
+    grad_hbm,
     update_ref,
     meshgrad_ref,
     hidden_ref,
@@ -60,6 +60,7 @@
     sendw_ref,
     recvw_ref,
     messw_ref,
+    gain_ref,
     latents,
     grads,
     hsums,
@@ -90,7 +91,7 @@
     chip = me // 2
     core = me % 2
     other = 1 - core
-    owned, width = latent_ref.shape
+    owned, width = latent_hbm.shape
     half = chips * owned
     nodes = 2 * half
     edges = terms.shape[1]
@@ -120,6 +121,8 @@
         pltpu.make_async_copy(source, target, load_sem.at[i])
         for i, (source, target) in enumerate(
             (
+                (latent_hbm, latents.at[core, chip]),
+                (grad_hbm, grads.at[core, chip]),
                 (embed_hbm, embed_ref),
                 (grid_hbm, grid_ref),
                 (sendw_hbm, sendw_ref),
@@ -127,13 +130,14 @@
                 (receiver_hbm, receiver_ref),
                 (recvw_hbm, recvw_ref),
                 (messw_hbm, messw_ref),
+                (gain_hbm, gain_ref),
             )
         )
     ]
     for load in loads:
         load.start()
-    latents[core, chip] = latent_ref[...]
-    grads[core, chip] = grad_ref[...]
+    loads[0].wait()
+    loads[1].wait()
 
     def chip_copy(slot, buffer, source, target):
         block = buffer.at[core, source]
@@ -176,18 +180,18 @@
         loop(0, lambda j: core_copy(slot, buffer, j, core).wait_send())
 
     def embed():
-        loads[0].wait()
-        loads[1].wait()
+        loads[2].wait()
+        loads[3].wait()
         embedded = dot_tn(grid_ref[...], embed_ref[...])
         embedded = (embedded * (0.5 * jnp.tanh(0.5 * embedded) + 0.5)).astype(BF16)
-        loads[2].wait()
+        loads[4].wait()
         table[...] = dot_nn(embedded, sendw_ref[...]).astype(BF16)
 
     pl.semaphore_wait(barrier, chips)
     spread_start(0, latents)
     embed()
-    loads[3].wait()
-    loads[4].wait()
+    loads[5].wait()
+    loads[6].wait()
 
     per_chunk = CHUNK // LANES
 
@@ -208,7 +212,7 @@
 
     chunks = edges // CHUNK
     lax.fori_loop(0, chunks, pick_senders, 0)
-    for load in loads[5:]:
+    for load in loads[7:]:
         load.wait()
     spread_forward(0, latents)
     spread_start(1, grads)
@@ -290,12 +294,12 @@
     own_hidden = collect(0).astype(BF16)
     hsums[core, chip] = own_hidden
     spread_start(2, hsums)
-    normed, agg = normalise(own_hidden, grad_ref[...])
-    update_ref[...] = (latent_ref[...].astype(F32) + normed * gain_ref[...]).astype(BF16)
+    normed, agg = normalise(own_hidden, grads[core, chip])
+    update_ref[...] = (latents[core, chip].astype(F32) + normed * gain_ref[...]).astype(BF16)
     hidden_grad = dot_nt(agg, messw_ref[...])
     spread_forward(2, hsums)
     recv_grad = (hidden_grad * collect(1)).astype(BF16)
-    meshgrad_ref[...] = (grad_ref[...].astype(F32) + dot_nt(recv_grad, recvw_ref[...])).astype(BF16)
+    meshgrad_ref[...] = (grads[core, chip].astype(F32) + dot_nt(recv_grad, recvw_ref[...])).astype(BF16)
     spread_finish(1, grads)
     spread_finish(2, hsums)
     every = hsums[...].reshape(nodes, width)
@@ -345,7 +349,7 @@
     update, mesh_grad, hidden, agg = pl.pallas_call(
         functools.partial(kernel, chips),
         out_shape=(row, row, every, every),
-        in_specs=[hbm, vmem, hbm, hbm, hbm, hbm, hbm, hbm, vmem, vmem],
+        in_specs=[hbm] * 10,
         out_specs=(vmem, vmem, vmem, vmem),
         scratch_shapes=[
             pltpu.VMEM((channels, senders), BF16),
@@ -355,6 +359,7 @@
             pltpu.VMEM((width, width), BF16),
             pltpu.VMEM((width, width), BF16),
             pltpu.VMEM((width, width), BF16),
+            pltpu.VMEM((1, width), F32),
             pltpu.VMEM(blocks, BF16),
             pltpu.VMEM(blocks, BF16),
             pltpu.VMEM(blocks, BF16),
@@ -370,7 +375,7 @@
             pltpu.VMEM(blocks, BF16),
             pltpu.VMEM(blocks, BF16),
             pltpu.VMEM(blocks, BF16),
-            dma((7,)),
+            dma((10,)),
             dma((3, chips)),
             dma((3, chips)),
             dma((3, chips)),
@@ -381,7 +386,7 @@
             dma((2, chips)),
         ],
         compiler_params=pltpu.CompilerParams(
-            collective_id=0, has_side_effects=True, vmem_limit_bytes=58 * 1024 * 1024
+            collective_id=0, has_side_effects=True, vmem_limit_bytes=61 * 1024 * 1024
         ),
     )(
         grid_inputs.T,

time: 33.3 us -> 32.6 us (0.979)
  Pallas kernels: 32.4 us -> 31.7 us
    pallas_call x1, Pallas kernels: 30 us -> 29.4 us  [shards(): pl.pallas_call(functools.partial(kernel, chips), out_shape=(row, row, eve...]
where the time goes in v3:
time: 32.6 us; the launch traced here: 32.4 us
  Pallas kernels  31.7 us (97%)
  between operations  0.64 us (2%)
    pallas_call x1, Pallas kernels, shards(): pl.pallas_call(functools.partial(kernel, chips), out_shape=(row, row, eve...  29.4 us
    pallas_call x1, Pallas kernels, shards(): pl.pallas_call(functools.partial(finish, 1.0 / math.sqrt(edges * n)), out...  2.36 us

profile of v3, /device:TPU:1, one launch (start us, length us, event | category | flops | bytes accessed | tf_op | source)
XLA Modules:
  0.0 32.4 jit_solution(14394617185480045593)
XLA Ops:
  0.6 29.4 %shard_map.121 = (bf16[16,512]{1,0:T(8,128)(2,1)}, bf16[16,512]{1,0:T(8,128)(2,1)}, bf16[256,512]{1,0:T(8,128)(2,1)}, bf16[256,512]{1,0:T(8,128)(2,1)}) custom-call(bf16[474,1024]{1,0:T(8,128)(2,1)} %bitcast.4, bf16[16,512]{1,0:T(8,128)(2,1)} %latent_hbm.1, s32[16,128]{1,0:T(8,128)} %bitcast.5, s32[16,128]{1,0:T(8,128)} %bitcast.6, ...), custom_call_target="tpu_custom_call" | custom-call | tf_op jit(solution)/shard_map/pallas_call | solution.py:349
  30.0 2.4 %shard_map.122 = (bf16[16,512]{1,0:T(8,128)(2,1)}, bf16[16,512]{1,0:T(8,128)(2,1)}, f32[512,512]{1,0:T(8,128)}) custom-call(bf16[16,512]{1,0:T(8,128)(2,1)} %get-tuple-element.7.update_in, bf16[16,512]{1,0:T(8,128)(2,1)} %get-tuple-element.8.meshgrad_in, bf16[256,512]{1,0:T(8,128)(2,1)} %get-tuple-element.9.hidden_ref, ...), custom_call_target="tpu_custom_call" | custom-call | tf_op jit(solution)/shard_map/pallas_call | solution.py:403

commit v4 on v3

--- a/solution.py
+++ b/solution.py
@@ -11,7 +11,7 @@
 LOGICAL = pl.DeviceIdType.MESH
 F32 = jnp.float32
 BF16 = jnp.bfloat16
-CHUNK = 512
+CHUNK = 1024
 LANES = 128
 
 

time: 32.6 us -> 32.4 us (level)
  no operation moved by 1% of the time
where the time goes in v4:
time: 32.4 us; the launch traced here: 32.1 us
  Pallas kernels  31.5 us (97%)
  between operations  0.64 us (2%)
    pallas_call x1, Pallas kernels, shards(): pl.pallas_call(functools.partial(kernel, chips), out_shape=(row, row, eve...  29.1 us
    pallas_call x1, Pallas kernels, shards(): pl.pallas_call(functools.partial(finish, 1.0 / math.sqrt(edges * n)), out...  2.36 us

profile of v4, /device:TPU:1, one launch (start us, length us, event | category | flops | bytes accessed | tf_op | source)
XLA Modules:
  0.0 32.1 jit_solution(3785709665655956825)
XLA Ops:
  0.6 29.1 %shard_map.121 = (bf16[16,512]{1,0:T(8,128)(2,1)}, bf16[16,512]{1,0:T(8,128)(2,1)}, bf16[256,512]{1,0:T(8,128)(2,1)}, bf16[256,512]{1,0:T(8,128)(2,1)}) custom-call(bf16[474,1024]{1,0:T(8,128)(2,1)} %bitcast.4, bf16[16,512]{1,0:T(8,128)(2,1)} %latent_hbm.1, s32[16,128]{1,0:T(8,128)} %bitcast.5, s32[16,128]{1,0:T(8,128)} %bitcast.6, ...), custom_call_target="tpu_custom_call" | custom-call | tf_op jit(solution)/shard_map/pallas_call | solution.py:349
  29.7 2.4 %shard_map.122 = (bf16[16,512]{1,0:T(8,128)(2,1)}, bf16[16,512]{1,0:T(8,128)(2,1)}, f32[512,512]{1,0:T(8,128)}) custom-call(bf16[16,512]{1,0:T(8,128)(2,1)} %get-tuple-element.7.update_in, bf16[16,512]{1,0:T(8,128)(2,1)} %get-tuple-element.8.meshgrad_in, bf16[256,512]{1,0:T(8,128)(2,1)} %get-tuple-element.9.hidden_ref, ...), custom_call_target="tpu_custom_call" | custom-call | tf_op jit(solution)/shard_map/pallas_call | solution.py:403
